TPU v7x, 32 devices: a whole 2x2x4 slice. The times are simulated.
32 devices in a mesh: groups: 1, gx: 8 (over z, y), gy: 2 (over core), segment: 2 (over x).
Axes of the slice: x: 2, y: 2, z: 4, core: 2. Of those that a mesh axis runs over, the one named last changes fastest.
Arguments:
- activations: bfloat16 [2, 8, 128, 128, 128], P('segment', 'groups', 'gx', 'gy'), may hold values from -6 to 6
- cotangent: bfloat16 [8, 128, 128, 128], P('groups', 'gx', 'gy'), may hold values from -6 to 6
- spectral_weights: float32 [2, 32, 32, 8, 8, 32], P('segment', 'gy', 'gx'), may hold values from -6 to 6
- pointwise: float32 [2, 8, 8], P('segment'), may hold values from -2 to 2
- channel_bias: float32 [2, 8], P('segment'), may hold values from -3 to 3
Outputs:
- input_grads: bfloat16 [2, 8, 128, 128, 128], P('segment', 'groups', 'gx', 'gy')
- spectral_grads: float32 [2, 32, 32, 8, 8, 32], P('segment', 'gy', 'gx', 'groups')
All inputs are finite; a program needn't handle non-finite values.
Results may differ from a plain program's by a relative error of at most 0.0042.
Values may be sent and summed in bfloat16 or wider, within the bound.
A program may use at most 64 MiB of HBM per device.

v0:
```python
import math
import jax
import jax.numpy as jnp
from jax import lax
from jax.sharding import PartitionSpec as P

MODES = 32
highest = lax.Precision.HIGHEST


def from_behind(block, axis, distance):
    devices = range(lax.axis_size(axis))
    route = [(i - distance, i) for i in devices if i - distance in devices]
    return lax.ppermute(block, axis, route)


def trig_basis(length, mode_count):
    half = mode_count // 2
    freqs = jnp.arange(half, dtype=jnp.int32)[:, None]
    points = jnp.arange(length, dtype=jnp.int32)[None, :]
    step_angle = 2.0 * math.pi / length
    cosine = jnp.cos((freqs * points % length).astype(jnp.float32) * step_angle)
    sine = jnp.sin(((freqs + 1) * points % length).astype(jnp.float32) * step_angle)
    rows_all = jnp.concatenate([cosine, sine], axis=0)
    scales = jnp.where(
        jnp.arange(mode_count) == 0, 1.0 / math.sqrt(length), math.sqrt(2.0 / length)
    ).astype(jnp.float32)
    return rows_all * scales[:, None]


def gelu_slope(value):
    normal_cdf = 0.5 * (1.0 + jax.scipy.special.erf(value * 0.7071067811865476))
    return normal_cdf + value * jnp.exp(-0.5 * value * value) * 0.3989422804014327


def channel_mix(matrix, field):
    return jnp.sum(matrix[:, :, None, None, None] * field[None], axis=1)


def body(activations, cotangent, spectral_weights, pointwise, channel_bias):
    inputs = activations[0].astype(jnp.float32)
    channels, rows_x, rows_y, length_z = inputs.shape
    count_x = lax.axis_size("gx")
    count_y = lax.axis_size("gy")
    mode_count = MODES
    along_x = trig_basis(rows_x * count_x, mode_count)
    along_z = trig_basis(length_z, mode_count)
    along_y = lax.dynamic_slice_in_dim(
        trig_basis(rows_y * count_y, mode_count), lax.axis_index("gy") * rows_y, rows_y, 1
    )
    weights = spectral_weights[0]
    mixing = pointwise[0]
    mixing_back = jnp.transpose(mixing)

    def analyse(field):
        third = jnp.einsum("ixyz,cz->cixy", field, along_z, precision=highest)
        partial_value = jnp.einsum(
            "cixy,ax->ciay",
            lax.all_to_all(third, "gx", split_axis=0, concat_axis=2, tiled=True),
            along_x,
            precision=highest,
        )
        return lax.psum_scatter(
            jnp.einsum("ciay,jy->jcia", partial_value, along_y, precision=highest),
            "gy",
            scatter_dimension=0,
            tiled=True,
        )

    def synthesise(spectrum):
        second = jnp.einsum(
            "jcia,jy->ciay",
            lax.all_gather(spectrum, "gy", axis=0, tiled=True),
            along_y,
            precision=highest,
        )
        spread = jnp.einsum("ciay,ax->cixy", second, along_x, precision=highest)
        return jnp.einsum(
            "cixy,cz->ixyz",
            lax.all_to_all(spread, "gx", split_axis=2, concat_axis=0, tiled=True),
            along_z,
            precision=highest,
        )

    input_modes = analyse(inputs)
    mixed = jnp.einsum("jcioa,jcia->jcoa", weights, input_modes, precision=highest)
    pre_act = channel_mix(mixing, inputs)
    pre_act = pre_act + channel_bias[0][:, None, None, None] + synthesise(mixed)
    slope_field = gelu_slope(pre_act)
    segment_index = lax.axis_index("segment")
    segment_count = lax.axis_size("segment")
    incoming = cotangent
    kept_grad = jnp.zeros(cotangent.shape, jnp.bfloat16)
    kept_modes = jnp.zeros(input_modes.shape, jnp.float32)
    for turn_index in range(segment_count):
        active = segment_index == segment_count - 1 - turn_index
        signal = incoming.astype(jnp.float32) * slope_field
        grad_modes = analyse(signal)
        back = jnp.einsum("jcioa,jcoa->jcia", weights, grad_modes, precision=highest)
        input_grad = channel_mix(mixing_back, signal) + synthesise(back)
        input_grad = input_grad.astype(jnp.bfloat16)
        kept_grad = jnp.where(active, input_grad, kept_grad)
        kept_modes = jnp.where(active, grad_modes, kept_modes)
        if turn_index + 1 < segment_count:
            incoming = from_behind(input_grad, "segment", -1)
    weight_grad = jnp.einsum("jcia,jcoa->jcioa", input_modes, kept_modes, precision=highest)
    return (kept_grad[None], weight_grad[None])


def solution(mesh):
    return jax.shard_map(
        body,
        mesh=mesh,
        in_specs=(
            P("segment", "groups", "gx", "gy", None),
            P("groups", "gx", "gy", None),
            P("segment", "gy", "gx", None, None, None),
            P("segment", None, None),
            P("segment", None),
        ),
        out_specs=(
            P("segment", "groups", "gx", "gy", None),
            P("segment", "gy", "gx", "groups", None, None),
        ),
        check_vma=False,
    )
```

profile of v0, /device:TPU:0, one launch (start us, length us, event | category | flops | bytes accessed | tf_op | source)
XLA Modules:
  0.0 441.0 jit_solution(13617722540841769567)
XLA Ops:
  7.4 7.4 %fusion.7 = f32[32,8,16,64]{3,0,2,1:T(8,128)S(1)} fusion(bf16[1,8,16,64,128]{4,3,2,1,0:T(8,128)(2,1)} %param.5, f32[32,128]{1,0:T(8,128)S(1)} %maximum_multiply_fusion), kind=kOutput, calls=%fused_computation.18 | convolution fusion | flops 402653184 | bytes 3162112 | tf_op jit(solution)/shard_map/ixyz,cz->cixy/dot_general | solution.py:56
  18.1 7.3 %all-to-all-start = ((f32[8,1,32768]{2,1,0:T(1,128)}), f32[8,1,32768]{2,1,0:T(1,128)S(1)}, u32[]{:S(2)}, u32[]{:S(2)}) async-start(f32[8,1,32768]{2,1,0:T(1,128)} %reshape.27), calls=%async_computation | async-start | bytes 2097152 | tf_op jit(solution)/shard_map/all_to_all | solution.py:59
  25.4 25.7 %all-to-all-done = f32[8,1,32768]{2,1,0:T(1,128)S(1)} async-done(((f32[8,1,32768]{2,1,0:T(1,128)}), f32[8,1,32768]{2,1,0:T(1,128)S(1)}, u32[]{:S(2)}, u32[]{:S(2)}) %all-to-all-start) | async-done | bytes 1048608 | tf_op jit(solution)/shard_map/all_to_all | solution.py:59
  60.4 7.1 %reduce-scatter.4.cloned.1.call-done = f32[16,4,8,32]{3,0,2,1:T(8,128)} async-done(((f32[32,4,8,32]{3,0,2,1:T(8,128)}), f32[16,4,8,32]{3,0,2,1:T(8,128)}) %reduce-scatter.4.cloned.1.call-update) | async-done | bytes 65552 | tf_op jit(solution)/shard_map/reduce_scatter | solution.py:63
  80.6 5.7 %all-to-all-start.1 = ((f32[8,1,32768]{2,1,0:T(1,128)}), f32[8,1,32768]{2,1,0:T(1,128)}, u32[]{:S(2)}, u32[]{:S(2)}) async-start(f32[8,1,32768]{2,1,0:T(1,128)} %reshape.29), calls=%async_computation.2 | async-start | bytes 2097152 | tf_op jit(solution)/shard_map/all_to_all | solution.py:80
  90.5 7.2 %multiply_reduce_fusion.2 = f32[8,16,64,128]{3,2,1,0:T(8,128)} fusion(f32[8,16,64,128]{3,2,1,0:T(8,128)} %bitcast_convert_fusion, f32[8,8]{1,0:T(8,128)S(1)} %bitcast.160), kind=kLoop, calls=%fused_computation.2 | loop fusion | flops 15728640 | bytes 8388864 | tf_op jit(solution)/shard_map/reduce_sum | solution.py:37
  97.6 15.1 %all-to-all-done.1 = f32[8,1,32768]{2,1,0:T(1,128)} async-done(((f32[8,1,32768]{2,1,0:T(1,128)}), f32[8,1,32768]{2,1,0:T(1,128)}, u32[]{:S(2)}, u32[]{:S(2)}) %all-to-all-start.1) | async-done | bytes 1048608 | tf_op jit(solution)/shard_map/all_to_all | solution.py:80
  112.8 4.3 reduce.7
  122.1 11.8 %convert_multiply_fusion.1 = (f32[8,16,64,128]{3,2,1,0:T(8,128)S(1)}, f32[8,16,64,128]{3,2,1,0:T(8,128)}) fusion(bf16[8,16,64,128]{3,2,1,0:T(8,128)(2,1)} %param.6, f32[32,8,16,64]{3,0,2,1:T(8,128)S(1)} %bitcast.153, f32[32,128]{1,0:T(8,128)S(1)} %maximum_multiply_fusion, f32[8,16,64,128]{3,2,1,0:T(8,128)S(1)} %copy-done.6, f32[8]{0:T(128)S(1)} %bitcast.162), kind=kOutput, calls=%fused_computation.11 | convolution fusion | flops 415236096 | bytes 15745056 | tf_op jit(solution)/shard_map/cixy,cz->ixyz/dot_general | solution.py:78
  133.9 11.3 %fusion.32 = f32[32,8,16,64]{3,0,2,1:T(8,128)S(1)} fusion(f32[8,16,64,128]{3,2,1,0:T(8,128)S(1)} %get-tuple-element.2, f32[32,128]{1,0:T(8,128)S(1)} %maximum_multiply_fusion), kind=kOutput, calls=%fused_computation.54 | convolution fusion | flops 402653184 | bytes 5259264 | tf_op jit(solution)/shard_map/ixyz,cz->cixy/dot_general | solution.py:56
  150.3 29.7 %all_to_all.108 = f32[8,1,32768]{2,1,0:T(1,128)} all-to-all(f32[8,1,32768]{2,1,0:T(1,128)S(1)} %reshape.31), channel_id=1, replica_groups=mesh['groups'=1,'gx'=8,'gy'=2,'segment'=2] {'gx'}, dimensions={0} | all-to-all | bytes 2097152 | tf_op jit(solution)/shard_map/all_to_all | solution.py:59
  192.8 7.1 %reduce-scatter.6.cloned.1.call-done = f32[16,4,8,32]{3,0,2,1:T(8,128)} async-done(((f32[32,4,8,32]{3,0,2,1:T(8,128)}), f32[16,4,8,32]{3,0,2,1:T(8,128)}) %reduce-scatter.6.cloned.1.call-update) | async-done | bytes 65552 | tf_op jit(solution)/shard_map/reduce_scatter | solution.py:63
  213.2 5.7 %all-to-all-start.3 = ((f32[8,1,32768]{2,1,0:T(1,128)}), f32[8,1,32768]{2,1,0:T(1,128)}, u32[]{:S(2)}, u32[]{:S(2)}) async-start(f32[8,1,32768]{2,1,0:T(1,128)} %reshape.33), calls=%async_computation.5 | async-start | bytes 2097152 | tf_op jit(solution)/shard_map/all_to_all | solution.py:80
  219.4 7.2 %multiply_reduce_fusion.1 = f32[8,16,64,128]{3,2,1,0:T(8,128)} fusion(f32[8,16,64,128]{3,2,1,0:T(8,128)} %copy-done.1, f32[8,8]{1,0:T(8,128)S(1)} %copy.49), kind=kLoop, calls=%fused_computation.1 | loop fusion | flops 15728640 | bytes 8388864 | tf_op jit(solution)/shard_map/reduce_sum | solution.py:37
  226.6 18.6 %all-to-all-done.3 = f32[8,1,32768]{2,1,0:T(1,128)} async-done(((f32[8,1,32768]{2,1,0:T(1,128)}), f32[8,1,32768]{2,1,0:T(1,128)}, u32[]{:S(2)}, u32[]{:S(2)}) %all-to-all-start.3) | async-done | bytes 1048608 | tf_op jit(solution)/shard_map/all_to_all | solution.py:80
  254.6 7.1 %add_convert_fusion.1 = bf16[8,16,64,128]{3,2,1,0:T(8,128)(2,1)S(1)} fusion(f32[8,16,64,128]{3,2,1,0:T(8,128)S(1)} %copy-done.4, f32[32,8,16,64]{3,0,2,1:T(8,128)S(1)} %bitcast.152, f32[32,128]{1,0:T(8,128)S(1)} %maximum_multiply_fusion), kind=kOutput, calls=%fused_computation.10 | convolution fusion | flops 404750336 | bytes 7356416 | tf_op jit(solution)/shard_map/cixy,cz->ixyz/dot_general | solution.py:78
  263.1 47.1 %collective-permute-done = bf16[8,16,64,128]{3,2,1,0:T(8,128)(2,1)S(1)} collective-permute-done((bf16[8,16,64,128]{3,2,1,0:T(8,128)(2,1)S(1)}, bf16[8,16,64,128]{3,2,1,0:T(8,128)(2,1)S(1)}, u32[]{:S(2)}, u32[]{:S(2)}) %collective-permute-start) | collective-permute-done | bytes 2097184 | tf_op jit(solution)/shard_map/ppermute | solution.py:14
  311.3 11.3 %fusion.27 = f32[32,8,16,64]{3,0,2,1:T(8,128)S(1)} fusion(f32[8,16,64,128]{3,2,1,0:T(8,128)S(1)} %convert_multiply_fusion, f32[32,128]{1,0:T(8,128)S(1)} %maximum_multiply_fusion), kind=kOutput, calls=%fused_computation.49 | convolution fusion | flops 402653184 | bytes 5259264 | tf_op jit(solution)/shard_map/ixyz,cz->cixy/dot_general | solution.py:56
  327.8 29.7 %all_to_all.109 = f32[8,1,32768]{2,1,0:T(1,128)} all-to-all(f32[8,1,32768]{2,1,0:T(1,128)S(1)} %reshape.35), channel_id=1, replica_groups=mesh['groups'=1,'gx'=8,'gy'=2,'segment'=2] {'gx'}, dimensions={0} | all-to-all | bytes 2097152 | tf_op jit(solution)/shard_map/all_to_all | solution.py:59
  370.4 6.1 %reduce-scatter.8.cloned.1.call-done = f32[16,4,8,32]{3,0,2,1:T(8,128)} async-done(((f32[32,4,8,32]{3,0,2,1:T(8,128)}), f32[16,4,8,32]{3,0,2,1:T(8,128)}) %reduce-scatter.8.cloned.1.call-update) | async-done | bytes 65552 | tf_op jit(solution)/shard_map/reduce_scatter | solution.py:63
  387.6 6.0 %all-to-all-start.5 = ((f32[8,1,32768]{2,1,0:T(1,128)}), f32[8,1,32768]{2,1,0:T(1,128)S(1)}, u32[]{:S(2)}, u32[]{:S(2)}) async-start(f32[8,1,32768]{2,1,0:T(1,128)} %reshape.37), calls=%async_computation.8 | async-start | bytes 2097152 | tf_op jit(solution)/shard_map/all_to_all | solution.py:80
  393.7 7.2 %multiply_reduce_fusion = f32[8,16,64,128]{3,2,1,0:T(8,128)} fusion(f32[8,16,64,128]{3,2,1,0:T(8,128)} %copy-done, f32[8,8]{1,0:T(8,128)S(1)} %copy.49), kind=kLoop, calls=%fused_computation | loop fusion | flops 15728640 | bytes 8388864 | tf_op jit(solution)/shard_map/reduce_sum | solution.py:37
  402.7 17.2 %all-to-all-done.5 = f32[8,1,32768]{2,1,0:T(1,128)S(1)} async-done(((f32[8,1,32768]{2,1,0:T(1,128)}), f32[8,1,32768]{2,1,0:T(1,128)S(1)}, u32[]{:S(2)}, u32[]{:S(2)}) %all-to-all-start.5) | async-done | bytes 1048608 | tf_op jit(solution)/shard_map/all_to_all | solution.py:80
  426.0 8.0 %select_bitcast_fusion = bf16[1,8,16,64,128]{4,3,2,1,0:T(8,128)(2,1)} fusion(bf16[8,16,64,128]{3,2,1,0:T(8,128)(2,1)} %copy-done.7, pred[]{:T(512)S(6)} %eq.24, pred[]{:T(512)S(6)} %eq.22, f32[8,16,64,128]{3,2,1,0:T(8,128)S(1)} %copy-done.3, f32[32,8,16,64]{3,0,2,1:T(8,128)S(1)} %bitcast.151, f32[32,128]{1,0:T(8,128)S(1)} %maximum_multiply_fusion), kind=kOutput, calls=%fused_computation.22 | convolution fusion | flops 406847488 | bytes 9453570 | tf_op jit(solution)/shard_map/cixy,cz->ixyz/dot_general | solution.py:78
  (92 shorter events, 115.1 us)
Async XLA Ops:
  18.1 33.0 %all-to-all-start = ((f32[8,1,32768]{2,1,0:T(1,128)}), f32[8,1,32768]{2,1,0:T(1,128)S(1)}, u32[]{:S(2)}, u32[]{:S(2)}) async-start(f32[8,1,32768]{2,1,0:T(1,128)} %reshape.27), calls=%async_computation | async-start | bytes 2097152 | tf_op jit(solution)/shard_map/all_to_all | solution.py:59
  25.4 42.1 %reduce-scatter.4.cloned.1.call-start = ((), (), s32[]{:S(2)}) async-start(), calls=%async_computation.9 | async-start | bytes 786432 | tf_op jit(solution)/shard_map/reduce_scatter | solution.py:63
  55.9 12.7 %copy-start.2 = (f32[1,16,4,8,8,32]{5,4,3,2,1,0:T(8,128)S(1)}, f32[1,16,4,8,8,32]{5,4,3,2,1,0:T(8,128)}, u32[]{:S(2)}) copy-start(f32[1,16,4,8,8,32]{5,4,3,2,1,0:T(8,128)} %param.7) | copy-start | bytes 1572868
  80.6 32.1 %all-to-all-start.1 = ((f32[8,1,32768]{2,1,0:T(1,128)}), f32[8,1,32768]{2,1,0:T(1,128)}, u32[]{:S(2)}, u32[]{:S(2)}) async-start(f32[8,1,32768]{2,1,0:T(1,128)} %reshape.29), calls=%async_computation.2 | async-start | bytes 2097152 | tf_op jit(solution)/shard_map/all_to_all | solution.py:80
  86.4 4.1 copy-start.10
  86.4 113.6 %reduce-scatter.6.cloned.1.call-start = ((), (), s32[]{:S(2)}) async-start(), calls=%async_computation.10 | async-start | bytes 786432 | tf_op jit(solution)/shard_map/reduce_scatter | solution.py:63
  119.2 2.8 copy-start.6
  119.2 2.8 copy-start.11
  133.9 11.4 %copy-start.1 = (f32[8,16,64,128]{3,2,1,0:T(8,128)}, f32[8,16,64,128]{3,2,1,0:T(8,128)S(1)}, u32[]{:S(2)}) copy-start(f32[8,16,64,128]{3,2,1,0:T(8,128)S(1)} %get-tuple-element.2) | copy-start | bytes 12582916
  213.2 32.1 %all-to-all-start.3 = ((f32[8,1,32768]{2,1,0:T(1,128)}), f32[8,1,32768]{2,1,0:T(1,128)}, u32[]{:S(2)}, u32[]{:S(2)}) async-start(f32[8,1,32768]{2,1,0:T(1,128)} %reshape.33), calls=%async_computation.5 | async-start | bytes 2097152 | tf_op jit(solution)/shard_map/all_to_all | solution.py:80
  218.9 157.6 %reduce-scatter.8.cloned.1.call-start = ((), (), s32[]{:S(2)}) async-start(), calls=%async_computation.11 | async-start | bytes 786432 | tf_op jit(solution)/shard_map/reduce_scatter | solution.py:63
  251.7 2.8 copy-start.4
  254.6 55.7 %copy-start.5 = (f32[8,16,64,128]{3,2,1,0:T(8,128)S(1)}, f32[8,16,64,128]{3,2,1,0:T(8,128)}, u32[]{:S(2)}) copy-start(f32[8,16,64,128]{3,2,1,0:T(8,128)} %get-tuple-element.3) | copy-start | bytes 12582916
  261.6 48.6 %copy-start.7 = (bf16[8,16,64,128]{3,2,1,0:T(8,128)(2,1)}, bf16[8,16,64,128]{3,2,1,0:T(8,128)(2,1)S(1)}, u32[]{:S(2)}) copy-start(bf16[8,16,64,128]{3,2,1,0:T(8,128)(2,1)S(1)} %add_convert_fusion.1) | copy-start | bytes 6291460
  261.6 48.6 %collective-permute-start = (bf16[8,16,64,128]{3,2,1,0:T(8,128)(2,1)S(1)}, bf16[8,16,64,128]{3,2,1,0:T(8,128)(2,1)S(1)}, u32[]{:S(2)}, u32[]{:S(2)}) collective-permute-start(bf16[8,16,64,128]{3,2,1,0:T(8,128)(2,1)S(1)} %add_convert_fusion.1), channel_id=1, source_target_pairs={{1,0},{3,2},{5,4},{7,6},{9,8},{11,10},{13,12},{15,14},{17,16},{19,... | collective-permute-start | bytes 6291464 | tf_op jit(solution)/shard_map/ppermute | solution.py:14
  311.3 11.4 %copy-start = (f32[8,16,64,128]{3,2,1,0:T(8,128)}, f32[8,16,64,128]{3,2,1,0:T(8,128)S(1)}, u32[]{:S(2)}) copy-start(f32[8,16,64,128]{3,2,1,0:T(8,128)S(1)} %convert_multiply_fusion) | copy-start | bytes 12582916
  387.6 32.3 %all-to-all-start.5 = ((f32[8,1,32768]{2,1,0:T(1,128)}), f32[8,1,32768]{2,1,0:T(1,128)S(1)}, u32[]{:S(2)}, u32[]{:S(2)}) async-start(f32[8,1,32768]{2,1,0:T(1,128)} %reshape.37), calls=%async_computation.8 | async-start | bytes 2097152 | tf_op jit(solution)/shard_map/all_to_all | solution.py:80
  393.7 7.2 %copy-start.8 = (f32[16,4,8,32]{3,0,2,1:T(8,128)S(1)}, f32[16,4,8,32]{3,0,2,1:T(8,128)}, u32[]{:S(2)}) copy-start(f32[16,4,8,32]{3,0,2,1:T(8,128)} %reduce-scatter.6.cloned.1.call-done) | copy-start | bytes 196612
  393.7 7.2 %copy-start.9 = (f32[16,4,8,32]{3,0,2,1:T(8,128)S(1)}, f32[16,4,8,32]{3,0,2,1:T(8,128)}, u32[]{:S(2)}) copy-start(f32[16,4,8,32]{3,0,2,1:T(8,128)} %reduce-scatter.8.cloned.1.call-done) | copy-start | bytes 196612
  423.8 2.2 copy-start.3
Sparse Core Ops, SparseCore 0:
  60.5 6.9 reduce-scatter.3
  193.0 6.9 reduce-scatter.5
  370.5 5.9 reduce-scatter.7
where the time goes:
time: 450 us; the launch traced here: 441 us
  waiting for transfers between devices  144 us (32%)
  matrix products  79.5 us (18%)
  blocking collectives  66.3 us (15%)
  local copies, waits for them, and re-layouts  55.7 us (12%)
  other arithmetic  53.9 us (12%)
  starting transfers between devices  26.8 us (6%)
  between operations  14.6 us (3%)
    all_to_all x2, blocking collectives, analyse(): lax.all_to_all(third, 'gx', split_axis=0, concat_axis=2, tiled=True)  59.4 us
    all_to_all x3, waiting for transfers between devices, synthesise(): lax.all_to_all(spread, 'gx', split_axis=2, concat_axis=0, tiled=True)  51 us
    ppermute x1, waiting for transfers between devices, from_behind(): return lax.ppermute(block, axis, route)  47.1 us
    unnamed x39, local copies, waits for them, and re-layouts  32.2 us
    dot_general x3, matrix products, analyse(): third = jnp.einsum('ixyz,cz->cixy', field, along_z, precision=highest)  30.1 us
    dot_general x3, matrix products, synthesise(): jnp.einsum('cixy,cz->ixyz', lax.all_to_all(spread, 'gx', split_axis=2, co...  26.9 us
    all_to_all x1, waiting for transfers between devices, analyse(): lax.all_to_all(third, 'gx', split_axis=0, concat_axis=2, tiled=True)  25.7 us
    reduce_sum x3, other arithmetic, channel_mix(): return jnp.sum(matrix[:, :, None, None, None] * field[None], axis=1)  21.6 us
  transfers between devices with their start and end apart: 8, of which 8 were waited for; matrix products, arithmetic and copies ran while one was open for 6% of the time, Pallas kernels for 0%

commit v1 on v0

--- a/solution.py
+++ b/solution.py
@@ -6,6 +6,13 @@
 
 MODES = 32
 highest = lax.Precision.HIGHEST
+
+
+def trade_parts(value, name, split, join):
+    size = lax.axis_size(name)
+    blocks = jnp.stack(jnp.split(value, size, axis=split), axis=0)
+    blocks = lax.all_to_all(blocks, name, split_axis=0, concat_axis=0)
+    return jnp.concatenate(blocks, axis=join)
 
 
 def from_behind(block, axis, distance):
@@ -76,10 +83,7 @@
         )
         spread = jnp.einsum("ciay,ax->cixy", second, along_x, precision=highest)
         return jnp.einsum(
-            "cixy,cz->ixyz",
-            lax.all_to_all(spread, "gx", split_axis=2, concat_axis=0, tiled=True),
-            along_z,
-            precision=highest,
+            "cixy,cz->ixyz", trade_parts(spread, "gx", 2, 0), along_z, precision=highest
         )
 
     input_modes = analyse(inputs)

time: 450 us -> 531 us (1.18)
  local copies, waits for them, and re-layouts: 55.7 us -> 135 us
    another operation x0 -> x30, local copies, waits for them, and re-layouts: none -> 64.2 us  [trade_parts(): blocks = jnp.stack(jnp.split(value, size, axis=split), axis=0)]
    unnamed x39 -> x86, local copies, waits for them, and re-layouts: 32.2 us -> 52.3 us
    transpose x3 -> x0, local copies, waits for them, and re-layouts: 7.47 us -> none  [synthesise(): spread = jnp.einsum('ciay,ax->cixy', second, along_x, precision=highest)]
  transfers between devices with their start and end apart: 8 -> 8, of which waited for: 8 -> 8; matrix products, arithmetic and copies ran while one was open for 6% -> 5% of each run, Pallas kernels for 0% -> 0%
where the time goes in v1:
time: 531 us; the launch traced here: 521 us
  waiting for transfers between devices  144 us (27%)
  local copies, waits for them, and re-layouts  135 us (25%)
  matrix products  79.6 us (15%)
  blocking collectives  66.9 us (13%)
  other arithmetic  54.3 us (10%)
  starting transfers between devices  26.7 us (5%)
  between operations  14.4 us (3%)
    another operation x30, local copies, waits for them, and re-layouts, trade_parts(): blocks = jnp.stack(jnp.split(value, size, axis=split), axis=0)  64.2 us
    all_to_all x2, blocking collectives, analyse(): lax.all_to_all(third, 'gx', split_axis=0, concat_axis=2, tiled=True)  59.8 us
    unnamed x86, local copies, waits for them, and re-layouts  52.3 us
    all_to_all x3, waiting for transfers between devices, trade_parts(): blocks = lax.all_to_all(blocks, name, split_axis=0, concat_axis=0)  51 us
    ppermute x1, waiting for transfers between devices, from_behind(): return lax.ppermute(block, axis, route)  47.1 us
    dot_general x3, matrix products, analyse(): third = jnp.einsum('ixyz,cz->cixy', field, along_z, precision=highest)  30.1 us
    dot_general x3, matrix products, synthesise(): jnp.einsum('cixy,cz->ixyz', trade_parts(spread, 'gx', 2, 0), along_z, pre...  27 us
    all_to_all x1, waiting for transfers between devices, analyse(): lax.all_to_all(third, 'gx', split_axis=0, concat_axis=2, tiled=True)  25.7 us
  transfers between devices with their start and end apart: 8, of which 8 were waited for; matrix products, arithmetic and copies ran while one was open for 5% of the time, Pallas kernels for 0%

profile of v1, /device:TPU:0, one launch (start us, length us, event | category | flops | bytes accessed | tf_op | source)
XLA Modules:
  0.0 521.2 jit_solution(13975355532718205358)
XLA Ops:
  7.4 7.4 %fusion.7 = f32[32,8,16,64]{3,0,2,1:T(8,128)S(1)} fusion(bf16[1,8,16,64,128]{4,3,2,1,0:T(8,128)(2,1)} %param.5, f32[32,128]{1,0:T(8,128)S(1)} %maximum_multiply_fusion), kind=kOutput, calls=%fused_computation.18 | convolution fusion | flops 402653184 | bytes 3162112 | tf_op jit(solution)/shard_map/ixyz,cz->cixy/dot_general | solution.py:63
  18.1 7.3 %all-to-all-start = ((f32[8,1,32768]{2,1,0:T(1,128)}), f32[8,1,32768]{2,1,0:T(1,128)S(1)}, u32[]{:S(2)}, u32[]{:S(2)}) async-start(f32[8,1,32768]{2,1,0:T(1,128)} %reshape.39), calls=%async_computation | async-start | bytes 2097152 | tf_op jit(solution)/shard_map/all_to_all | solution.py:66
  25.4 25.7 %all-to-all-done = f32[8,1,32768]{2,1,0:T(1,128)S(1)} async-done(((f32[8,1,32768]{2,1,0:T(1,128)}), f32[8,1,32768]{2,1,0:T(1,128)S(1)}, u32[]{:S(2)}, u32[]{:S(2)}) %all-to-all-start) | async-done | bytes 1048608 | tf_op jit(solution)/shard_map/all_to_all | solution.py:66
  60.5 7.1 %reduce-scatter.4.cloned.1.call-done = f32[16,4,8,32]{3,0,2,1:T(8,128)} async-done(((f32[32,4,8,32]{3,0,2,1:T(8,128)}), f32[16,4,8,32]{3,0,2,1:T(8,128)}) %reduce-scatter.4.cloned.1.call-update) | async-done | bytes 65552 | tf_op jit(solution)/shard_map/reduce_scatter | solution.py:70
  109.6 5.7 %all-to-all-start.1 = ((f32[8,1,32768]{2,1,0:T(1,128)}), f32[8,1,32768]{2,1,0:T(1,128)}, u32[]{:S(2)}, u32[]{:S(2)}) async-start(f32[8,1,32768]{2,1,0:T(1,128)} %reshape.41), calls=%async_computation.2 | async-start | bytes 2097152 | tf_op jit(solution)/shard_map/all_to_all | solution.py:14
  119.6 7.2 %multiply_reduce_fusion.2 = f32[8,16,64,128]{3,2,1,0:T(8,128)} fusion(f32[8,16,64,128]{3,2,1,0:T(8,128)} %bitcast_convert_fusion, f32[8,8]{1,0:T(8,128)S(1)} %bitcast.187), kind=kLoop, calls=%fused_computation.2 | loop fusion | flops 15728640 | bytes 8388864 | tf_op jit(solution)/shard_map/reduce_sum | solution.py:44
  126.7 14.9 %all-to-all-done.1 = f32[8,1,32768]{2,1,0:T(1,128)} async-done(((f32[8,1,32768]{2,1,0:T(1,128)}), f32[8,1,32768]{2,1,0:T(1,128)}, u32[]{:S(2)}, u32[]{:S(2)}) %all-to-all-start.1) | async-done | bytes 1048608 | tf_op jit(solution)/shard_map/all_to_all | solution.py:14
  151.3 11.9 %convert_multiply_fusion.1 = (f32[8,16,64,128]{3,2,1,0:T(8,128)S(1)}, f32[8,16,64,128]{3,2,1,0:T(8,128)}) fusion(bf16[8,16,64,128]{3,2,1,0:T(8,128)(2,1)} %param.6, f32[32,8,16,64]{3,0,2,1:T(8,128)S(1)} %bitcast.180, f32[32,128]{1,0:T(8,128)S(1)} %maximum_multiply_fusion, f32[8,16,64,128]{3,2,1,0:T(8,128)S(1)} %copy-done.6, f32[8]{0:T(128)S(1)} %bitcast.189), kind=kOutput, calls=%fused_computation.11 | convolution fusion | flops 415236096 | bytes 15745056 | tf_op jit(solution)/shard_map/cixy,cz->ixyz/dot_general | solution.py:85
  163.2 11.3 %fusion.32 = f32[32,8,16,64]{3,0,2,1:T(8,128)S(1)} fusion(f32[8,16,64,128]{3,2,1,0:T(8,128)S(1)} %get-tuple-element.26, f32[32,128]{1,0:T(8,128)S(1)} %maximum_multiply_fusion), kind=kOutput, calls=%fused_computation.102 | convolution fusion | flops 402653184 | bytes 5259264 | tf_op jit(solution)/shard_map/ixyz,cz->cixy/dot_general | solution.py:63
  179.7 29.9 %all_to_all.69 = f32[8,1,32768]{2,1,0:T(1,128)} all-to-all(f32[8,1,32768]{2,1,0:T(1,128)S(1)} %reshape.43), channel_id=1, replica_groups=mesh['groups'=1,'gx'=8,'gy'=2,'segment'=2] {'gx'}, dimensions={0} | all-to-all | bytes 2097152 | tf_op jit(solution)/shard_map/all_to_all | solution.py:66
  222.5 7.1 %reduce-scatter.6.cloned.1.call-done = f32[16,4,8,32]{3,0,2,1:T(8,128)} async-done(((f32[32,4,8,32]{3,0,2,1:T(8,128)}), f32[16,4,8,32]{3,0,2,1:T(8,128)}) %reduce-scatter.6.cloned.1.call-update) | async-done | bytes 65552 | tf_op jit(solution)/shard_map/reduce_scatter | solution.py:70
  236.7 5.0 slice_bitcast_fusion.8
  271.6 5.8 %all-to-all-start.3 = ((f32[8,1,32768]{2,1,0:T(1,128)}), f32[8,1,32768]{2,1,0:T(1,128)}, u32[]{:S(2)}, u32[]{:S(2)}) async-start(f32[8,1,32768]{2,1,0:T(1,128)} %reshape.45), calls=%async_computation.5 | async-start | bytes 2097152 | tf_op jit(solution)/shard_map/all_to_all | solution.py:14
  277.6 7.2 %multiply_reduce_fusion.1 = f32[8,16,64,128]{3,2,1,0:T(8,128)} fusion(f32[8,16,64,128]{3,2,1,0:T(8,128)} %copy-done.1, f32[8,8]{1,0:T(8,128)S(1)} %copy.64), kind=kLoop, calls=%fused_computation.1 | loop fusion | flops 15728640 | bytes 8388864 | tf_op jit(solution)/shard_map/reduce_sum | solution.py:44
  284.8 18.9 %all-to-all-done.3 = f32[8,1,32768]{2,1,0:T(1,128)} async-done(((f32[8,1,32768]{2,1,0:T(1,128)}), f32[8,1,32768]{2,1,0:T(1,128)}, u32[]{:S(2)}, u32[]{:S(2)}) %all-to-all-start.3) | async-done | bytes 1048608 | tf_op jit(solution)/shard_map/all_to_all | solution.py:14
  313.3 7.1 %add_convert_fusion.1 = bf16[8,16,64,128]{3,2,1,0:T(8,128)(2,1)S(1)} fusion(f32[8,16,64,128]{3,2,1,0:T(8,128)S(1)} %copy-done.4, f32[32,8,16,64]{3,0,2,1:T(8,128)S(1)} %bitcast.179, f32[32,128]{1,0:T(8,128)S(1)} %maximum_multiply_fusion), kind=kOutput, calls=%fused_computation.10 | convolution fusion | flops 404750336 | bytes 7356416 | tf_op jit(solution)/shard_map/cixy,cz->ixyz/dot_general | solution.py:85
  321.9 47.1 %collective-permute-done = bf16[8,16,64,128]{3,2,1,0:T(8,128)(2,1)S(1)} collective-permute-done((bf16[8,16,64,128]{3,2,1,0:T(8,128)(2,1)S(1)}, bf16[8,16,64,128]{3,2,1,0:T(8,128)(2,1)S(1)}, u32[]{:S(2)}, u32[]{:S(2)}) %collective-permute-start) | collective-permute-done | bytes 2097184 | tf_op jit(solution)/shard_map/ppermute | solution.py:21
  370.1 11.3 %fusion.27 = f32[32,8,16,64]{3,0,2,1:T(8,128)S(1)} fusion(f32[8,16,64,128]{3,2,1,0:T(8,128)S(1)} %convert_multiply_fusion, f32[32,128]{1,0:T(8,128)S(1)} %maximum_multiply_fusion), kind=kOutput, calls=%fused_computation.97 | convolution fusion | flops 402653184 | bytes 5259264 | tf_op jit(solution)/shard_map/ixyz,cz->cixy/dot_general | solution.py:63
  386.6 29.9 %all_to_all.70 = f32[8,1,32768]{2,1,0:T(1,128)} all-to-all(f32[8,1,32768]{2,1,0:T(1,128)S(1)} %reshape.47), channel_id=1, replica_groups=mesh['groups'=1,'gx'=8,'gy'=2,'segment'=2] {'gx'}, dimensions={0} | all-to-all | bytes 2097152 | tf_op jit(solution)/shard_map/all_to_all | solution.py:66
  429.4 6.1 %reduce-scatter.8.cloned.1.call-done = f32[16,4,8,32]{3,0,2,1:T(8,128)} async-done(((f32[32,4,8,32]{3,0,2,1:T(8,128)}), f32[16,4,8,32]{3,0,2,1:T(8,128)}) %reduce-scatter.8.cloned.1.call-update) | async-done | bytes 65552 | tf_op jit(solution)/shard_map/reduce_scatter | solution.py:70
  468.0 6.0 %all-to-all-start.5 = ((f32[8,1,32768]{2,1,0:T(1,128)}), f32[8,1,32768]{2,1,0:T(1,128)S(1)}, u32[]{:S(2)}, u32[]{:S(2)}) async-start(f32[8,1,32768]{2,1,0:T(1,128)} %reshape.49), calls=%async_computation.8 | async-start | bytes 2097152 | tf_op jit(solution)/shard_map/all_to_all | solution.py:14
  474.0 7.2 %multiply_reduce_fusion = f32[8,16,64,128]{3,2,1,0:T(8,128)} fusion(f32[8,16,64,128]{3,2,1,0:T(8,128)} %copy-done, f32[8,8]{1,0:T(8,128)S(1)} %copy.64), kind=kLoop, calls=%fused_computation | loop fusion | flops 15728640 | bytes 8388864 | tf_op jit(solution)/shard_map/reduce_sum | solution.py:44
  483.0 17.2 %all-to-all-done.5 = f32[8,1,32768]{2,1,0:T(1,128)S(1)} async-done(((f32[8,1,32768]{2,1,0:T(1,128)}), f32[8,1,32768]{2,1,0:T(1,128)S(1)}, u32[]{:S(2)}, u32[]{:S(2)}) %all-to-all-start.5) | async-done | bytes 1048608 | tf_op jit(solution)/shard_map/all_to_all | solution.py:14
  506.4 8.0 %select_bitcast_fusion = bf16[1,8,16,64,128]{4,3,2,1,0:T(8,128)(2,1)} fusion(bf16[8,16,64,128]{3,2,1,0:T(8,128)(2,1)} %copy-done.7, pred[]{:T(512)S(6)} %eq.24, pred[]{:T(512)S(6)} %eq.22, f32[8,16,64,128]{3,2,1,0:T(8,128)S(1)} %copy-done.3, f32[32,8,16,64]{3,0,2,1:T(8,128)S(1)} %bitcast.178, f32[32,128]{1,0:T(8,128)S(1)} %maximum_multiply_fusion), kind=kOutput, calls=%fused_computation.22 | convolution fusion | flops 406847488 | bytes 9453570 | tf_op jit(solution)/shard_map/cixy,cz->ixyz/dot_general | solution.py:85
  (166 shorter events, 194.2 us)
Async XLA Ops:
  18.1 33.0 %all-to-all-start = ((f32[8,1,32768]{2,1,0:T(1,128)}), f32[8,1,32768]{2,1,0:T(1,128)S(1)}, u32[]{:S(2)}, u32[]{:S(2)}) async-start(f32[8,1,32768]{2,1,0:T(1,128)} %reshape.39), calls=%async_computation | async-start | bytes 2097152 | tf_op jit(solution)/shard_map/all_to_all | solution.py:66
  25.4 42.3 %reduce-scatter.4.cloned.1.call-start = ((), (), s32[]{:S(2)}) async-start(), calls=%async_computation.9 | async-start | bytes 786432 | tf_op jit(solution)/shard_map/reduce_scatter | solution.py:70
  56.0 12.7 %copy-start.2 = (f32[1,16,4,8,8,32]{5,4,3,2,1,0:T(8,128)S(1)}, f32[1,16,4,8,8,32]{5,4,3,2,1,0:T(8,128)}, u32[]{:S(2)}) copy-start(f32[1,16,4,8,8,32]{5,4,3,2,1,0:T(8,128)} %param.7) | copy-start | bytes 1572868
  96.5 6.8 %copy-start.18 = (f32[1,4,8,16,64]{4,3,2,1,0:T(8,128)S(1)}, f32[1,4,8,16,64]{4,3,2,1,0:T(8,128)}, u32[]{:S(2)}) copy-start(f32[1,4,8,16,64]{4,3,2,1,0:T(8,128)} %copy.73) | copy-start | bytes 393220
  96.5 7.5 %copy-start.15 = (f32[1,4,8,16,64]{4,3,2,1,0:T(8,128)S(1)}, f32[1,4,8,16,64]{4,3,2,1,0:T(8,128)}, u32[]{:S(2)}) copy-start(f32[1,4,8,16,64]{4,3,2,1,0:T(8,128)} %copy.74) | copy-start | bytes 393220
  96.5 8.2 %copy-start.12 = (f32[1,4,8,16,64]{4,3,2,1,0:T(8,128)S(1)}, f32[1,4,8,16,64]{4,3,2,1,0:T(8,128)}, u32[]{:S(2)}) copy-start(f32[1,4,8,16,64]{4,3,2,1,0:T(8,128)} %copy.75) | copy-start | bytes 393220
  96.5 9.0 %copy-start.9 = (f32[1,4,8,16,64]{4,3,2,1,0:T(8,128)S(1)}, f32[1,4,8,16,64]{4,3,2,1,0:T(8,128)}, u32[]{:S(2)}) copy-start(f32[1,4,8,16,64]{4,3,2,1,0:T(8,128)} %copy.76) | copy-start | bytes 393220
  109.6 32.1 %all-to-all-start.1 = ((f32[8,1,32768]{2,1,0:T(1,128)}), f32[8,1,32768]{2,1,0:T(1,128)}, u32[]{:S(2)}, u32[]{:S(2)}) async-start(f32[8,1,32768]{2,1,0:T(1,128)} %reshape.41), calls=%async_computation.2 | async-start | bytes 2097152 | tf_op jit(solution)/shard_map/all_to_all | solution.py:14
  115.3 114.4 %reduce-scatter.6.cloned.1.call-start = ((), (), s32[]{:S(2)}) async-start(), calls=%async_computation.10 | async-start | bytes 786432 | tf_op jit(solution)/shard_map/reduce_scatter | solution.py:70
  163.2 11.4 %copy-start.1 = (f32[8,16,64,128]{3,2,1,0:T(8,128)}, f32[8,16,64,128]{3,2,1,0:T(8,128)S(1)}, u32[]{:S(2)}) copy-start(f32[8,16,64,128]{3,2,1,0:T(8,128)S(1)} %get-tuple-element.26) | copy-start | bytes 12582916
  258.5 6.8 %copy-start.19 = (f32[1,4,8,16,64]{4,3,2,1,0:T(8,128)S(1)}, f32[1,4,8,16,64]{4,3,2,1,0:T(8,128)}, u32[]{:S(2)}) copy-start(f32[1,4,8,16,64]{4,3,2,1,0:T(8,128)} %copy.86) | copy-start | bytes 393220
  258.5 7.5 %copy-start.16 = (f32[1,4,8,16,64]{4,3,2,1,0:T(8,128)S(1)}, f32[1,4,8,16,64]{4,3,2,1,0:T(8,128)}, u32[]{:S(2)}) copy-start(f32[1,4,8,16,64]{4,3,2,1,0:T(8,128)} %copy.87) | copy-start | bytes 393220
  258.5 8.2 %copy-start.13 = (f32[1,4,8,16,64]{4,3,2,1,0:T(8,128)S(1)}, f32[1,4,8,16,64]{4,3,2,1,0:T(8,128)}, u32[]{:S(2)}) copy-start(f32[1,4,8,16,64]{4,3,2,1,0:T(8,128)} %copy.88) | copy-start | bytes 393220
  258.5 9.0 %copy-start.10 = (f32[1,4,8,16,64]{4,3,2,1,0:T(8,128)S(1)}, f32[1,4,8,16,64]{4,3,2,1,0:T(8,128)}, u32[]{:S(2)}) copy-start(f32[1,4,8,16,64]{4,3,2,1,0:T(8,128)} %copy.89) | copy-start | bytes 393220
  271.6 32.1 %all-to-all-start.3 = ((f32[8,1,32768]{2,1,0:T(1,128)}), f32[8,1,32768]{2,1,0:T(1,128)}, u32[]{:S(2)}, u32[]{:S(2)}) async-start(f32[8,1,32768]{2,1,0:T(1,128)} %reshape.45), calls=%async_computation.5 | async-start | bytes 2097152 | tf_op jit(solution)/shard_map/all_to_all | solution.py:14
  277.3 158.3 %reduce-scatter.8.cloned.1.call-start = ((), (), s32[]{:S(2)}) async-start(), calls=%async_computation.11 | async-start | bytes 786432 | tf_op jit(solution)/shard_map/reduce_scatter | solution.py:70
  313.3 55.7 %copy-start.5 = (f32[8,16,64,128]{3,2,1,0:T(8,128)S(1)}, f32[8,16,64,128]{3,2,1,0:T(8,128)}, u32[]{:S(2)}) copy-start(f32[8,16,64,128]{3,2,1,0:T(8,128)} %get-tuple-element.27) | copy-start | bytes 12582916
  320.4 48.6 %copy-start.7 = (bf16[8,16,64,128]{3,2,1,0:T(8,128)(2,1)}, bf16[8,16,64,128]{3,2,1,0:T(8,128)(2,1)S(1)}, u32[]{:S(2)}) copy-start(bf16[8,16,64,128]{3,2,1,0:T(8,128)(2,1)S(1)} %add_convert_fusion.1) | copy-start | bytes 6291460
  320.4 48.6 %collective-permute-start = (bf16[8,16,64,128]{3,2,1,0:T(8,128)(2,1)S(1)}, bf16[8,16,64,128]{3,2,1,0:T(8,128)(2,1)S(1)}, u32[]{:S(2)}, u32[]{:S(2)}) collective-permute-start(bf16[8,16,64,128]{3,2,1,0:T(8,128)(2,1)S(1)} %add_convert_fusion.1), channel_id=1, source_target_pairs={{1,0},{3,2},{5,4},{7,6},{9,8},{11,10},{13,12},{15,14},{17,16},{19,... | collective-permute-start | bytes 6291464 | tf_op jit(solution)/shard_map/ppermute | solution.py:21
  370.1 11.4 %copy-start = (f32[8,16,64,128]{3,2,1,0:T(8,128)}, f32[8,16,64,128]{3,2,1,0:T(8,128)S(1)}, u32[]{:S(2)}) copy-start(f32[8,16,64,128]{3,2,1,0:T(8,128)S(1)} %convert_multiply_fusion) | copy-start | bytes 12582916
  451.8 6.9 %copy-start.8 = (f32[1,4,8,16,64]{3,4,2,1,0:T(8,128)S(1)}, f32[1,4,8,16,64]{3,4,2,1,0:T(8,128)}, u32[]{:S(2)}) copy-start(f32[1,4,8,16,64]{3,4,2,1,0:T(8,128)} %get-tuple-element.7) | copy-start | bytes 393220
  468.0 32.2 %all-to-all-start.5 = ((f32[8,1,32768]{2,1,0:T(1,128)}), f32[8,1,32768]{2,1,0:T(1,128)S(1)}, u32[]{:S(2)}, u32[]{:S(2)}) async-start(f32[8,1,32768]{2,1,0:T(1,128)} %reshape.49), calls=%async_computation.8 | async-start | bytes 2097152 | tf_op jit(solution)/shard_map/all_to_all | solution.py:14
  474.0 7.2 %copy-start.21 = (f32[16,4,8,32]{3,0,2,1:T(8,128)S(1)}, f32[16,4,8,32]{3,0,2,1:T(8,128)}, u32[]{:S(2)}) copy-start(f32[16,4,8,32]{3,0,2,1:T(8,128)} %reduce-scatter.6.cloned.1.call-done) | copy-start | bytes 196612
  474.0 7.2 %copy-start.22 = (f32[16,4,8,32]{3,0,2,1:T(8,128)S(1)}, f32[16,4,8,32]{3,0,2,1:T(8,128)}, u32[]{:S(2)}) copy-start(f32[16,4,8,32]{3,0,2,1:T(8,128)} %reduce-scatter.8.cloned.1.call-done) | copy-start | bytes 196612
  (9 other events, 34.8 us)
Sparse Core Ops, SparseCore 0:
  60.7 6.9 reduce-scatter.3
  222.6 6.9 reduce-scatter.5
  429.5 5.9 reduce-scatter.7
